TPU v7x, 32 devices: a whole 2x2x4 slice. The times are simulated.
32 devices in a mesh: blk: 8 (over z, y), lev: 4 (over x, core).
Axes of the slice: x: 2, y: 2, z: 4, core: 2. Of those that a mesh axis runs over, the one named last changes fastest.
Arguments:
- adjoint_in: float32 [512, 12, 1024], P('blk', 'lev'), may hold values from -6 to 6
- courant: float32 [2, 512, 12, 1024], P(None, 'blk', 'lev'), may hold values from 0.05 to 0.45
- mixing: float32 [512, 12, 1024], P('blk', 'lev'), may hold values from 0.5 to 8
- oh_rate: float32 [512, 12, 1024], P('blk', 'lev'), may hold values from 0.02 to 0.6
- substeps: int32 [512], P('blk'), may hold values from 1 to 4
- nest_weight: float32 [512, 128], P('blk'), may hold values from 0.2 to 0.9
- dest_device: int32 [512, 1], P('blk'), may hold values from 0 to 7; in each aligned block of 64 rows (0 to 63, 64 to 127, ...) at most 16 rows name the same one
- dest_slot: int32 [512], P('blk'), may hold values from 0 to 63
- emission_profile: float32 [12], P('lev'), may hold values from 0.05 to 1
- tile_owner: int32 [512], P('blk'), may hold values from 0 to 127, as said below
Outputs:
- adjoint_out: float32 [512, 12, 1024], P('blk', 'lev')
- tile_grad: float32 [128, 1024], P(('blk', 'lev'))
Inputs may be any that keep to these rules, and one draw needn't show every extreme that they name: Of the 64 blocks of one index of blk, at most 16 have the same dest_device. Tiles form 8 groups of 16 consecutive tiles. Of the 64 blocks of one index of blk, at most 16 have tile_owner in the same group, and some group holds exactly 16 of them.
All inputs are finite; a program needn't handle non-finite values.
Results may differ from a plain program's by a relative error of at most 0.0003.
Values sent between devices are 32-bit elements; how exact they have to be, the bound alone decides.
A program may use at most 128 MiB of HBM per device.

v0:
```python
import jax
import jax.numpy as jnp
from jax import lax
from jax.sharding import PartitionSpec as P

RMAX = 4
STEPS = 2


def solve_columns(right_side, coupling):
    level_count = right_side.shape[1]
    ratios = []
    scaled = []
    for level in range(level_count):
        lower_k = coupling[:, level - 1] if level > 0 else 0.0
        upper_k = coupling[:, level] if level < level_count - 1 else 0.0
        diag_term = 1.0 + lower_k + upper_k
        if level == 0:
            pivot_val = diag_term
            scaled.append(right_side[:, 0] / pivot_val)
        else:
            pivot_val = diag_term + lower_k * ratios[level - 1]
            scaled.append((right_side[:, level] + lower_k * scaled[level - 1]) / pivot_val)
        ratios.append(-upper_k / pivot_val)
    solved = [None] * level_count
    solved[level_count - 1] = scaled[level_count - 1]
    for level in range(level_count - 2, -1, -1):
        solved[level] = scaled[level] - ratios[level] * solved[level + 1]
    return jnp.stack(solved, axis=1)


def stencil(adjoint, east_u, north_u, side_len):
    shape_grid = adjoint.shape[:-1] + (side_len, side_len)
    grid_view = adjoint.reshape(shape_grid)
    east_c = east_u.reshape(shape_grid)
    north_c = north_u.reshape(shape_grid)
    zero_col = jnp.zeros(shape_grid[:-1] + (1,), jnp.float32)
    east_adj = jnp.concatenate([grid_view[..., 1:], zero_col], axis=-1)
    zero_row = jnp.zeros(shape_grid[:-2] + (1, side_len), jnp.float32)
    north_adj = jnp.concatenate([grid_view[..., 1:, :], zero_row], axis=-2)
    result = (1.0 - east_c - north_c) * grid_view + east_c * east_adj + north_c * north_adj
    return result.reshape(adjoint.shape)


def faces(adjoint, side_len):
    grid_view = adjoint.reshape(adjoint.shape[:-1] + (side_len, side_len))
    return jnp.concatenate(
        [
            grid_view[..., 0, :],
            grid_view[..., side_len - 1, :],
            grid_view[..., :, 0],
            grid_view[..., :, side_len - 1],
        ],
        axis=-1,
    )


def add_faces(adjoint, arrivals, side_len):
    grid_view = adjoint.reshape(adjoint.shape[:-1] + (side_len, side_len))
    grid_view = grid_view.at[..., 0, :].add(arrivals[..., 0:side_len])
    grid_view = grid_view.at[..., side_len - 1, :].add(arrivals[..., side_len : 2 * side_len])
    grid_view = grid_view.at[..., :, 0].add(arrivals[..., 2 * side_len : 3 * side_len])
    grid_view = grid_view.at[..., :, side_len - 1].add(arrivals[..., 3 * side_len :])
    return grid_view.reshape(adjoint.shape)


def route_cycles(cycle_flat, key_float, own_keys):
    all_cycles, all_keys = (
        lax.all_gather(cycle_flat, "blk", axis=0, tiled=True),
        lax.all_gather(key_float[:, None], "blk", axis=0, tiled=True),
    )
    picking = (all_keys[:, 0][None, :] == own_keys[:, None]).astype(jnp.float32)
    return jnp.dot(picking, all_cycles, precision=lax.Precision.HIGHEST)


def local(
    adjoint_in,
    courant,
    mixing,
    oh_rate,
    substeps,
    nest_weight,
    dest_device,
    dest_slot,
    emission_profile,
    tile_owner,
):
    blocks, lev_dev, cell_count = adjoint_in.shape
    cycle_len = nest_weight.shape[1]
    side_len = cycle_len // 4
    peer_count = lax.axis_size("blk")
    lev_groups = lax.axis_size("lev")
    my_block = lax.axis_index("blk")
    survive = jnp.exp(-oh_rate)
    dest_index = dest_device[:, 0]
    key_float = (dest_index * blocks + dest_slot + 1).astype(jnp.float32)
    own_keys = (my_block * blocks + jnp.arange(blocks, dtype=jnp.int32) + 1).astype(jnp.float32)
    column_mixing = lax.all_to_all(mixing, "lev", split_axis=2, concat_axis=1, tiled=True)
    adjoint = adjoint_in
    grad_sum = jnp.zeros((blocks, cell_count), jnp.float32)
    for step_index in range(STEPS):
        grad_sum = grad_sum + jnp.sum(adjoint * emission_profile[None, :, None], axis=1)
        columns = lax.all_to_all(adjoint * survive, "lev", split_axis=2, concat_axis=1, tiled=True)
        solved = solve_columns(columns, column_mixing)
        adjoint = lax.all_to_all(solved, "lev", split_axis=1, concat_axis=2, tiled=True)
        cycle_out = faces(adjoint, side_len) * nest_weight[:, None, :]
        arrivals = route_cycles(cycle_out.reshape(blocks, -1), key_float, own_keys)
        arrivals = arrivals.reshape(cycle_out.shape)
        advected = adjoint
        for substep in range(RMAX):
            active = (substep < substeps)[:, None, None]
            advected = jnp.where(
                active, stencil(advected, courant[0], courant[1], side_len), advected
            )
        adjoint = add_faces(advected, arrivals, side_len)
    tiles_total = blocks * peer_count // 4
    tile_rows = jnp.arange(
        lax.axis_size(("blk", "lev")) * (tiles_total // (peer_count * lev_groups)), dtype=jnp.int32
    )
    tile_hot = (tile_owner[None, :] == tile_rows[:, None]).astype(jnp.float32)
    tile_grad = lax.psum_scatter(
        jnp.dot(tile_hot, grad_sum, precision=lax.Precision.HIGHEST),
        ("blk", "lev"),
        scatter_dimension=0,
        tiled=True,
    )
    return (adjoint, tile_grad)


def solution(mesh):
    placed = (
        P("blk", "lev", None),
        P(None, "blk", "lev", None),
        P("blk", "lev", None),
        P("blk", "lev", None),
        P("blk"),
        P("blk", None),
        P("blk", None),
        P("blk"),
        P("lev"),
        P("blk"),
    )
    return jax.shard_map(
        local,
        mesh=mesh,
        in_specs=placed,
        out_specs=(P("blk", "lev", None), P(("blk", "lev"), None)),
        check_vma=False,
    )
```

profile of v0, /device:TPU:0, one launch (start us, length us, event | category | flops | bytes accessed | tf_op | source)
XLA Modules:
  0.0 417.6 jit_solution(15685037477598765283)
XLA Ops:
  10.4 2.6 reshape.375
  13.0 4.2 %all-to-all-start = ((f32[4,1,49152]{2,1,0:T(1,128)}), f32[4,1,49152]{2,1,0:T(1,128)S(1)}, u32[]{:S(2)}, u32[]{:S(2)}) async-start(f32[4,1,49152]{2,1,0:T(1,128)} %reshape.375), calls=%async_computation | async-start | bytes 1572864 | tf_op jit(solution)/shard_map/all_to_all | solution.py:103
  19.0 2.6 reshape.373
  21.6 7.3 %all-to-all-done = f32[4,1,49152]{2,1,0:T(1,128)S(1)} async-done(((f32[4,1,49152]{2,1,0:T(1,128)}), f32[4,1,49152]{2,1,0:T(1,128)S(1)}, u32[]{:S(2)}, u32[]{:S(2)}) %all-to-all-start) | async-done | bytes 786464 | tf_op jit(solution)/shard_map/all_to_all | solution.py:103
  28.8 4.2 %all-to-all-start.1 = ((f32[4,1,49152]{2,1,0:T(1,128)}), f32[4,1,49152]{2,1,0:T(1,128)}, u32[]{:S(2)}, u32[]{:S(2)}) async-start(f32[4,1,49152]{2,1,0:T(1,128)} %reshape.373), calls=%async_computation.1 | async-start | bytes 1572864 | tf_op jit(solution)/shard_map/all_to_all | solution.py:98
  33.5 3.8 reduce.18
  41.1 3.6 all-to-all-done.1
  44.7 3.8 reduce.17
  63.2 4.2 %all-to-all-start.2 = ((f32[64,12,256]{2,0,1:T(8,128)}), f32[64,12,256]{2,0,1:T(8,128)}, u32[]{:S(2)}, u32[]{:S(2)}) async-start(f32[64,12,256]{2,0,1:T(8,128)} %constant_dynamic-update-slice_fusion), calls=%async_computation.2 | async-start | bytes 1572864 | tf_op jit(solution)/shard_map/all_to_all | solution.py:105
  73.4 22.5 %all-reduce.16 = f32[512]{0:T(512)S(1)} all-reduce(f32[512]{0:T(512)S(1)} %fusion.43), channel_id=2, replica_groups=mesh['blk'=8,'lev'=4] {'blk'}, use_global_device_ids=true, to_apply=%add.16 | all-reduce | flops 512 | bytes 4096
  96.0 2.8 copy.165
  111.1 32.2 %all_gather.11 = f32[512,384]{1,0:T(8,128)S(1)} all-gather(f32[64,384]{1,0:T(8,128)S(1)} %copy.193), channel_id=1, replica_groups=mesh['blk'=8,'lev'=4] {'blk'}, dimensions={0}, use_global_device_ids=true | all-gather | bytes 884736 | tf_op jit(solution)/shard_map/all_gather | solution.py:69
  151.5 3.3 add_select_fusion.4
  156.1 2.7 scatter-add.30
  159.9 2.7 scatter-add.31
  162.7 2.7 copy.173
  167.8 2.7 copy.174
  170.5 4.3 %reshape.377 = f32[4,1,49152]{2,1,0:T(1,128)} reshape(f32[1024,3,64]{2,1,0:T(4,128)} %bitcast.128) | data formatting | bytes 1572864
  174.8 4.4 %all-to-all-start.3 = ((f32[4,1,49152]{2,1,0:T(1,128)}), f32[4,1,49152]{2,1,0:T(1,128)}, u32[]{:S(2)}, u32[]{:S(2)}) async-start(f32[4,1,49152]{2,1,0:T(1,128)} %reshape.377), calls=%async_computation.3 | async-start | bytes 1572864 | tf_op jit(solution)/shard_map/all_to_all | solution.py:103
  179.2 2.5 multiply_reduce_fusion
  183.7 7.0 %all-to-all-done.3 = f32[4,1,49152]{2,1,0:T(1,128)} async-done(((f32[4,1,49152]{2,1,0:T(1,128)}), f32[4,1,49152]{2,1,0:T(1,128)}, u32[]{:S(2)}, u32[]{:S(2)}) %all-to-all-start.3) | async-done | bytes 786464 | tf_op jit(solution)/shard_map/all_to_all | solution.py:103
  190.7 4.7 %reduce.19 = f32[4,49152]{1,0:T(4,128)} reduce(f32[4,1,49152]{2,1,0:T(1,128)} %all-to-all-done.3, f32[]{:T(128)} %broadcast.551), dimensions={1}, to_apply=%all_to_all.72.reduce_sub_computation | reduce | bytes 1572868 | tf_op jit(solution)/shard_map/all_to_all | solution.py:103
  195.4 3.7 reshape.378
  199.1 2.6 copy.176
  213.9 4.2 %all-to-all-start.4 = ((f32[64,12,256]{2,0,1:T(8,128)}), f32[64,12,256]{2,0,1:T(8,128)}, u32[]{:S(2)}, u32[]{:S(2)}) async-start(f32[64,12,256]{2,0,1:T(8,128)} %constant_dynamic-update-slice_fusion.11), calls=%async_computation.4 | async-start | bytes 1572864 | tf_op jit(solution)/shard_map/all_to_all | solution.py:105
  220.4 129.4 %all-reduce.20.cloned.1.call-done = f32[128,1024]{1,0:T(8,128)} async-done(((f32[128,1024]{1,0:T(8,128)}), f32[128,1024]{1,0:T(8,128)}) %all-reduce.20.cloned.1.call-update) | async-done | bytes 524304
  351.2 2.8 copy.177
  364.0 32.5 %all_gather.12 = f32[512,384]{1,0:T(8,128)S(1)} all-gather(f32[64,384]{1,0:T(8,128)S(1)} %copy.196), channel_id=1, replica_groups=mesh['blk'=8,'lev'=4] {'blk'}, dimensions={0}, use_global_device_ids=true | all-gather | bytes 884736 | tf_op jit(solution)/shard_map/all_gather | solution.py:69
  397.4 2.9 add_select_fusion
  401.5 2.8 scatter-add.36
  405.3 2.7 scatter-add.39
  408.1 2.7 copy.188
  (171 shorter events, 85.1 us)
Async XLA Ops:
  13.0 15.9 %all-to-all-start = ((f32[4,1,49152]{2,1,0:T(1,128)}), f32[4,1,49152]{2,1,0:T(1,128)S(1)}, u32[]{:S(2)}, u32[]{:S(2)}) async-start(f32[4,1,49152]{2,1,0:T(1,128)} %reshape.375), calls=%async_computation | async-start | bytes 1572864 | tf_op jit(solution)/shard_map/all_to_all | solution.py:103
  28.8 15.9 %all-to-all-start.1 = ((f32[4,1,49152]{2,1,0:T(1,128)}), f32[4,1,49152]{2,1,0:T(1,128)}, u32[]{:S(2)}, u32[]{:S(2)}) async-start(f32[4,1,49152]{2,1,0:T(1,128)} %reshape.373), calls=%async_computation.1 | async-start | bytes 1572864 | tf_op jit(solution)/shard_map/all_to_all | solution.py:98
  50.5 11.3 %copy-start.5 = (f32[64,4,3,256]{3,0,2,1:T(8,128)}, f32[64,4,3,256]{3,0,2,1:T(8,128)S(1)}, u32[]{:S(2)}) copy-start(f32[64,4,3,256]{3,0,2,1:T(8,128)S(1)} %copy.164) | copy-start | bytes 2359300
  52.7 4.3 %copy-start.8 = (f32[64,1,256]{2,0,1:T(8,128)}, f32[64,1,256]{2,0,1:T(8,128)S(1)}, u32[]{:S(2)}) copy-start(f32[64,1,256]{2,0,1:T(8,128)S(1)} %get-tuple-element.150) | copy-start | bytes 196612
  52.7 4.3 %copy-start.10 = (f32[64,1,256]{2,0,1:T(8,128)}, f32[64,1,256]{2,0,1:T(8,128)S(1)}, u32[]{:S(2)}) copy-start(f32[64,1,256]{2,0,1:T(8,128)S(1)} %get-tuple-element.134) | copy-start | bytes 196612
  52.7 4.3 %copy-start.12 = (f32[64,1,256]{2,0,1:T(8,128)}, f32[64,1,256]{2,0,1:T(8,128)S(1)}, u32[]{:S(2)}) copy-start(f32[64,1,256]{2,0,1:T(8,128)S(1)} %get-tuple-element.139) | copy-start | bytes 196612
  52.8 4.3 %copy-start.14 = (f32[64,1,256]{2,0,1:T(8,128)}, f32[64,1,256]{2,0,1:T(8,128)S(1)}, u32[]{:S(2)}) copy-start(f32[64,1,256]{2,0,1:T(8,128)S(1)} %get-tuple-element.144) | copy-start | bytes 196612
  52.8 4.3 %copy-start.16 = (f32[64,1,256]{2,0,1:T(8,128)}, f32[64,1,256]{2,0,1:T(8,128)S(1)}, u32[]{:S(2)}) copy-start(f32[64,1,256]{2,0,1:T(8,128)S(1)} %get-tuple-element.149) | copy-start | bytes 196612
  52.8 4.3 %copy-start.18 = (f32[64,1,256]{2,0,1:T(8,128)}, f32[64,1,256]{2,0,1:T(8,128)S(1)}, u32[]{:S(2)}) copy-start(f32[64,1,256]{2,0,1:T(8,128)S(1)} %get-tuple-element.154) | copy-start | bytes 196612
  63.2 32.8 %all-to-all-start.2 = ((f32[64,12,256]{2,0,1:T(8,128)}), f32[64,12,256]{2,0,1:T(8,128)}, u32[]{:S(2)}, u32[]{:S(2)}) async-start(f32[64,12,256]{2,0,1:T(8,128)} %constant_dynamic-update-slice_fusion), calls=%async_computation.2 | async-start | bytes 1572864 | tf_op jit(solution)/shard_map/all_to_all | solution.py:105
  67.4 2.5 copy-start.25
  70.0 39.4 %copy-start.20 = (f32[64,128]{0,1:T(8,128)}, f32[64,128]{0,1:T(8,128)S(1)}, u32[]{:S(2)}) copy-start(f32[64,128]{0,1:T(8,128)S(1)} %copy.167) | copy-start | bytes 98308
  70.4 2.8 copy-start.33
  70.5 2.8 copy-start.34
  70.5 25.5 %copy-start.32 = (s32[64]{0:T(128)S(1)}, s32[64]{0:T(128)}, u32[]{:S(2)}) copy-start(s32[64]{0:T(128)} %param.30) | copy-start | bytes 772
  96.0 47.3 %copy-start.28 = (f32[64]{0:T(128)}, f32[64]{0:T(128)S(1)}, u32[]{:S(2)}) copy-start(f32[64]{0:T(128)S(1)} %add_convert_fusion) | copy-start | bytes 772
  96.0 6.7 %copy-start.26 = (pred[64]{0:T(512)(128)(4,1)}, pred[64]{0:T(512)(128)(4,1)S(1)}, u32[]{:S(2)}) copy-start(pred[64]{0:T(512)(128)(4,1)S(1)} %get-tuple-element.175) | copy-start | bytes 196
  99.6 2.8 copy-start.1
  106.5 2.9 copy-start.2
  151.5 3.3 copy-start.24
  151.5 4.5 %copy-start.23 = (f32[64,3,32]{0,2,1:T(8,128)S(1)}, f32[64,3,32]{0,2,1:T(8,128)}, u32[]{:S(2)}) copy-start(f32[64,3,32]{0,2,1:T(8,128)} %copy.201) | copy-start | bytes 73732
  170.5 8.7 %copy-start.30 = (f32[3]{0:T(128)S(1)}, f32[3]{0:T(128)}, u32[]{:S(2)}) copy-start(f32[3]{0:T(128)} %param.34) | copy-start | bytes 40
  174.8 15.9 %all-to-all-start.3 = ((f32[4,1,49152]{2,1,0:T(1,128)}), f32[4,1,49152]{2,1,0:T(1,128)}, u32[]{:S(2)}, u32[]{:S(2)}) async-start(f32[4,1,49152]{2,1,0:T(1,128)} %reshape.377), calls=%async_computation.3 | async-start | bytes 1572864 | tf_op jit(solution)/shard_map/all_to_all | solution.py:103
  199.1 2.6 copy-start.11
  199.1 2.6 copy-start.13
  201.7 1.7 copy-start.17
  207.7 10.4 %copy-start.31 = (s32[64]{0:T(128)S(1)}, s32[64]{0:T(128)}, u32[]{:S(2)}) copy-start(s32[64]{0:T(128)} %param.35) | copy-start | bytes 772
  213.9 137.3 %all-to-all-start.4 = ((f32[64,12,256]{2,0,1:T(8,128)}), f32[64,12,256]{2,0,1:T(8,128)}, u32[]{:S(2)}, u32[]{:S(2)}) async-start(f32[64,12,256]{2,0,1:T(8,128)} %constant_dynamic-update-slice_fusion.11), calls=%async_computation.4 | async-start | bytes 1572864 | tf_op jit(solution)/shard_map/all_to_all | solution.py:105
  218.1 131.7 %all-reduce.20.cloned.1.call-start = ((), (), s32[]{:S(2)}) async-start(), calls=%async_computation.5 | async-start | bytes 1048576
  356.0 1.9 copy-start
  363.9 32.6 %copy-start.29 = (f32[64]{0:T(128)S(1)}, f32[64]{0:T(128)}, u32[]{:S(2)}) copy-start(f32[64]{0:T(128)} %copy-done.28) | copy-start | bytes 772
  364.0 33.3 %slice-start = ((f32[64,3,32,32]{0,3,2,1:T(8,128)}), f32[64,3,31,32]{0,3,2,1:T(8,128)S(1)}, s32[]{:S(2)}) async-start(f32[64,3,32,32]{0,3,2,1:T(8,128)} %copy-done.3), calls=%async_computation.6 | async-start | bytes 3047424 | tf_op jit(solution)/shard_map/slice | solution.py:40
  (11 other events, 16.6 us)
Sparse Core Ops, SparseCore 0:
  224.2 125.5 all-reduce.19
where the time goes:
time: 420 us; the launch traced here: 418 us
  waiting for transfers between devices  147 us (35%)
  local copies, waits for them, and re-layouts  89.2 us (21%)
  blocking collectives  87.2 us (21%)
  other arithmetic  53.3 us (13%)
  starting transfers between devices  21.2 us (5%)
  between operations  15.3 us (4%)
    unnamed x2, waiting for transfers between devices  129 us
    all_gather x2, blocking collectives, route_cycles(): lax.all_gather(cycle_flat, 'blk', axis=0, tiled=True)  64.7 us
    unnamed x98, local copies, waits for them, and re-layouts  37.3 us
    unnamed x1, blocking collectives  22.5 us
    all_to_all x2, waiting for transfers between devices, local(): lax.all_to_all(adjoint * survive, 'lev', split_axis=2, concat_axis=1, til...  14.3 us
    select_n x8, other arithmetic, local(): jnp.where(active, stencil(advected, courant[0], courant[1], side_len), ad...  12.1 us
    unnamed x13, other arithmetic  11.6 us
    all_to_all x2, starting transfers between devices, local(): lax.all_to_all(adjoint * survive, 'lev', split_axis=2, concat_axis=1, til...  8.61 us
  transfers between devices with their start and end apart: 6, of which 4 were waited for; matrix products, arithmetic and copies ran while one was open for 6% of the time, Pallas kernels for 0%

commit v1 on v0

v1 whole, which is shorter than its diff:
```python
import functools

import jax
import jax.numpy as jnp
from jax import lax
from jax.experimental import pallas as pl
from jax.experimental.pallas import tpu as pltpu
from jax.sharding import PartitionSpec as P

RMAX = 4
STEPS = 2
CHUNKS = 4
GROUP = 8
MESH = pl.DeviceIdType.MESH
F32 = jnp.float32
BF16 = jnp.bfloat16


def split_dot(left, right, dims=((1,), (0,))):
    def run(a, b):
        return lax.dot_general(a, b, (dims, ((), ())), preferred_element_type=F32)

    if left.dtype == BF16:
        high = right.astype(BF16)
        low = (right - high.astype(F32)).astype(BF16)
        return run(left, high) + run(left, low)
    high = left.astype(BF16)
    low = (left - high.astype(F32)).astype(BF16)
    return run(high, right) + run(low, right)


def each(count, body):
    if count <= 16:
        for off in range(1, count):
            body(off)
    else:
        lax.fori_loop(1, count, lambda off, c: (body(off), c)[1], 0)


def kernel(
    peers,
    levs,
    adj,
    courant,
    mix,
    oh,
    ints,
    weight,
    profile,
    out,
    tile_out,
    surv,
    centre,
    east,
    north,
    x,
    coef,
    middle,
    grad,
    gather_t,
    spread_t,
    pick,
    place,
    flat,
    key_send,
    key_recv,
    face_send,
    face_recv,
    line_send,
    line_recv,
    cross_send,
    cross_recv,
    back_send,
    back_recv,
    tiles,
    tiles_recv,
    owned,
    owned_recv,
    line_ss,
    line_rs,
    cross_ss,
    cross_rs,
    back_ss,
    back_rs,
    key_ss,
    key_rs,
    face_ss,
    face_rs,
    tile_ss,
    tile_rs,
    own_ss,
    own_rs,
):
    lev_here, blocks, cells = adj.shape
    cycle = weight.shape[1]
    side = cycle // 4
    cap = key_send.shape[1]
    slots = peers * cap
    chunk = blocks // CHUNKS
    my_blk = lax.axis_index("blk")
    my_lev = lax.axis_index("lev")
    lower = my_lev < 2
    outer = jnp.logical_or(my_lev == 0, my_lev == levs - 1)

    def peer_at(off):
        return lax.rem(my_blk + off, peers)

    def source_at(off):
        return lax.rem(my_blk + peers - off, peers)

    barrier = pltpu.get_barrier_semaphore()
    each(peers, lambda off: pl.semaphore_signal(
        barrier, inc=1, device_id=(peer_at(off), my_lev), device_id_type=MESH))
    for off in range(1, levs):
        pl.semaphore_signal(
            barrier, inc=1, device_id=(my_blk, lax.rem(my_lev + off, levs)), device_id_type=MESH)

    def rows_of(part, item):
        return pl.ds(pl.multiple_of(part * chunk + item * GROUP, GROUP), GROUP)

    def level_at(p):
        return jnp.where(lower, p, lev_here - 1 - p)

    def link_at(p):
        return jnp.where(lower, p, lev_here - 2 - p)

    def link_pair(d, k, flag):
        inv = 1.0 / (d + k)
        return jnp.where(flag, inv, 0.0), jnp.where(flag, k * inv, 1.0)

    last = lev_here - 1

    def line_copy(step, part, target):
        return pltpu.make_async_remote_copy(
            line_send.at[step, part], line_recv.at[step, part],
            line_ss.at[step, part], line_rs.at[step, part],
            device_id=(my_blk, target), device_id_type=MESH)

    def first_line(part, target):
        return pltpu.make_async_remote_copy(
            line_send.at[STEPS, part], line_recv.at[STEPS, part],
            line_ss.at[STEPS, part], line_rs.at[STEPS, part],
            device_id=(my_blk, target), device_id_type=MESH)

    def cross_copy(step, part, target):
        return pltpu.make_async_remote_copy(
            cross_send.at[step, part], cross_recv.at[step, part],
            cross_ss.at[step, part], cross_rs.at[step, part],
            device_id=(my_blk, target), device_id_type=MESH)

    def back_copy(step, part, target):
        return pltpu.make_async_remote_copy(
            back_send.at[step, part], back_recv.at[step, part],
            back_ss.at[step, part], back_rs.at[step, part],
            device_id=(my_blk, target), device_id_type=MESH)

    partner = jnp.where(lower, 1 - my_lev, 5 - my_lev)
    across = 3 - my_lev

    def forward(step, rows, d, f):
        for p in range(lev_here):
            if p > 0:
                c = coef[2 * (p - 1), rows, :]
                f = x[level_at(p), rows, :] * surv[level_at(p), rows, :] + c * f
            x[level_at(p), rows, :] = f
            if step == 0:
                if p > 0:
                    d = 1.0 + c * d
                if p < last:
                    k = mix[link_at(p), rows, :]
                    inv = 1.0 / (d + k)
                    coef[2 * p, rows, :] = k * inv
                    coef[2 * p + 1, rows, :] = inv
        return d, f

    def backward(rows, value):
        x[level_at(last), rows, :] = value
        for p in range(last - 1, -1, -1):
            value = x[level_at(p), rows, :] * coef[2 * p + 1, rows, :] + coef[2 * p, rows, :] * value
            x[level_at(p), rows, :] = value
        return value

    items = chunk // GROUP
    end_c, end_i = 2 * last, 2 * last + 1

    def send_rows(item):
        return pl.ds(pl.multiple_of(item * GROUP, GROUP), GROUP)

    def solve(step):
        @pl.when(outer)
        def _():
            for part in range(CHUNKS):
                @pl.loop(0, items)
                def _(item):
                    rows, own = rows_of(part, item), send_rows(item)
                    d, f = forward(
                        step, rows, jnp.ones((GROUP, cells), F32),
                        x[level_at(0), rows, :] * surv[level_at(0), rows, :])
                    if step == 0:
                        inv, c = link_pair(d, mix[last, rows, :], lower)
                        coef[end_c, rows, :] = c
                        coef[end_i, rows, :] = inv
                        line_send[STEPS, part, own, :] = c * d
                    else:
                        c = coef[end_c, rows, :]
                    line_send[step, part, own, :] = c * f

                if step == 0:
                    first_line(part, partner).start()
                line_copy(step, part, partner).start()
            for part in range(CHUNKS):
                back_copy(step, part, partner).wait_recv()

                @pl.loop(0, items)
                def _(item):
                    rows, own = rows_of(part, item), send_rows(item)
                    value = x[level_at(last), rows, :] * coef[end_i, rows, :]
                    value = value + coef[end_c, rows, :] * back_recv[step, part, own, :]
                    backward(rows, value)

        @pl.when(jnp.logical_not(outer))
        def _():
            for part in range(CHUNKS):
                if step == 0:
                    first_line(part, partner).wait_recv()
                line_copy(step, part, partner).wait_recv()

                @pl.loop(0, items)
                def _(item):
                    rows, own = rows_of(part, item), send_rows(item)
                    f_in = line_recv[step, part, own, :]
                    d = None
                    if step == 0:
                        d_in = line_recv[STEPS, part, own, :]
                        inv, c_in = link_pair(
                            d_in, mix[last, rows, :], jnp.logical_not(lower))
                        middle[0, rows, :] = inv
                        middle[1, rows, :] = c_in
                        d = 1.0 + c_in * d_in
                    else:
                        c_in = middle[1, rows, :]
                    d, f = forward(
                        step, rows, d,
                        x[level_at(0), rows, :] * surv[level_at(0), rows, :] + c_in * f_in)
                    if step == 0:
                        _, c = link_pair(d, mix[last, rows, :], lower)
                        coef[end_c, rows, :] = c
                        coef[end_i, rows, :] = d
                        cross_send[STEPS, part, own, :] = c * d
                    else:
                        c = coef[end_c, rows, :]
                    cross_send[step, part, own, :] = c * f

                if step == 0:
                    cross_copy(STEPS, part, across).start()
                cross_copy(step, part, across).start()
            for part in range(CHUNKS):
                if step == 0:
                    cross_copy(STEPS, part, across).wait_recv()
                cross_copy(step, part, across).wait_recv()

                @pl.loop(0, items)
                def _(item):
                    rows, own = rows_of(part, item), send_rows(item)
                    if step == 0:
                        d_in = cross_recv[STEPS, part, own, :]
                        _, c_in = link_pair(d_in, mix[last, rows, :], lower)
                        inv = 1.0 / (coef[end_i, rows, :] + c_in * d_in)
                        middle[2, rows, :] = c_in
                        middle[3, rows, :] = inv
                    else:
                        c_in = middle[2, rows, :]
                        inv = middle[3, rows, :]
                    value = (x[level_at(last), rows, :] + c_in * cross_recv[step, part, own, :]) * inv
                    value = backward(rows, value)
                    back_send[step, part, own, :] = (
                        middle[0, rows, :] * line_recv[step, part, own, :]
                        + middle[1, rows, :] * value)

                back_copy(step, part, partner).start()

    def finish_solve(step):
        @pl.when(outer)
        def _():
            for part in range(CHUNKS):
                if step == 0:
                    first_line(part, partner).wait_send()
                line_copy(step, part, partner).wait_send()

        @pl.when(jnp.logical_not(outer))
        def _():
            for part in range(CHUNKS):
                if step == 0:
                    cross_copy(STEPS, part, across).wait_send()
                cross_copy(step, part, across).wait_send()
                back_copy(step, part, partner).wait_send()

    def key_copy(off, whose):
        return pltpu.make_async_remote_copy(
            key_send.at[peer_at(off)], key_recv.at[whose], key_ss.at[off], key_rs.at[off],
            device_id=(peer_at(off), my_lev), device_id_type=MESH)

    def face_copy(step, off, whose):
        return pltpu.make_async_remote_copy(
            face_send.at[step, peer_at(off)], face_recv.at[step, whose],
            face_ss.at[step, off], face_rs.at[step, off],
            device_id=(peer_at(off), my_lev), device_id_type=MESH)

    def tile_copy(off, whose):
        target = lax.rem(my_lev + off, levs)
        return pltpu.make_async_remote_copy(
            tiles.at[target], tiles_recv.at[whose], tile_ss.at[off], tile_rs.at[off],
            device_id=(my_blk, target), device_id_type=MESH)

    def own_copy(off, whose):
        return pltpu.make_async_remote_copy(
            owned.at[peer_at(off)], owned_recv.at[whose], own_ss.at[off], own_rs.at[off],
            device_id=(peer_at(off), my_lev), device_id_type=MESH)

    def split_rows(value, target):
        width = value.shape[1]
        if cap % 8 == 0:
            target[...] = value.reshape(peers, cap, width)
        else:
            flat[:, :width] = value
            for p in range(peers):
                target[p] = flat[p * cap : (p + 1) * cap, :width]

    def join_rows(source):
        width = source.shape[-1]
        if cap % 8 == 0:
            return source[...].reshape(slots, width)
        for p in range(peers):
            flat[p * cap : (p + 1) * cap, :width] = source[p]
        return flat[:, :width]

    @pl.loop(0, blocks // GROUP)
    def _(item):
        rows = pl.ds(pl.multiple_of(item * GROUP, GROUP), GROUP)
        for level in range(lev_here):
            surv[level, rows, :] = jnp.exp(-oh[level, rows, :])
            x[level, rows, :] = adj[level, rows, :]

    pl.semaphore_wait(barrier, peers - 1 + levs - 1)

    def prepare():
        eye = (
            lax.broadcasted_iota(jnp.int32, (blocks, blocks), 0)
            == lax.broadcasted_iota(jnp.int32, (blocks, blocks), 1)
        )

        def column(row):
            return jnp.sum(jnp.where(eye, row, 0.0), axis=1, keepdims=True)

        dest = ints[1:2, :]
        same = jnp.logical_and(
            column(dest) == dest,
            lax.broadcasted_iota(jnp.int32, (blocks, blocks), 0)
            < lax.broadcasted_iota(jnp.int32, (blocks, blocks), 1),
        )
        rank = jnp.sum(jnp.where(same, 1.0, 0.0), axis=0, keepdims=True)
        slot_row = dest * cap + rank
        slot_id = lax.broadcasted_iota(jnp.int32, (slots, blocks), 0).astype(F32)
        pick[...] = jnp.where(slot_id == slot_row, 1.0, 0.0).astype(BF16)
        keys = column(ints[2:3, :]) + jnp.zeros((blocks, 128), F32)
        split_rows(
            jnp.dot(pick[...], keys.astype(BF16), preferred_element_type=F32), key_send)
        key_recv[my_blk] = key_send[my_blk]
        each(peers, lambda off: key_copy(off, my_blk).start())

        face = lax.broadcasted_iota(jnp.int32, (cycle, cells), 0)
        cell = lax.broadcasted_iota(jnp.int32, (cycle, cells), 1)
        wanted = jnp.where(
            face < side, face,
            jnp.where(
                face < 2 * side, face + (cells - 2 * side),
                jnp.where(
                    face < 3 * side, (face - 2 * side) * side,
                    (face - 3 * side) * side + side - 1)))
        spread_t[...] = jnp.where(cell == wanted, 1.0, 0.0).astype(BF16)
        face = lax.broadcasted_iota(jnp.int32, (cells, cycle), 1)
        cell = lax.broadcasted_iota(jnp.int32, (cells, cycle), 0)
        wanted = jnp.where(
            face < side, face,
            jnp.where(
                face < 2 * side, face + (cells - 2 * side),
                jnp.where(
                    face < 3 * side, (face - 2 * side) * side,
                    (face - 3 * side) * side + side - 1)))
        gather_t[...] = jnp.where(cell == wanted, 1.0, 0.0).astype(BF16)

        @pl.loop(0, blocks // GROUP)
        def _(item):
            rows = pl.ds(pl.multiple_of(item * GROUP, GROUP), GROUP)
            cell = lax.broadcasted_iota(jnp.int32, (GROUP, cells), 1)
            total = jnp.zeros((GROUP, cells), F32)
            for level in range(lev_here):
                e, n = courant[0, level, rows, :], courant[1, level, rows, :]
                centre[level, rows, :] = 1.0 - e - n
                east[level, rows, :] = jnp.where(cell % side == side - 1, 0.0, e)
                north[level, rows, :] = jnp.where(cell >= cells - side, 0.0, n)
                total = total + profile[level] * adj[level, rows, :]
            grad[rows, :] = total

        return column(ints[0:1, :])

    solve(0)
    sub_column = prepare()
    sub_wide = sub_column + jnp.zeros((blocks, 128), F32)
    place_ready = False
    flat_sub = sub_wide

    for step in range(STEPS):
        if step > 0:
            solve(step)
        cyc = [
            split_dot(x[level], gather_t[...]) * weight[...] for level in range(lev_here)
        ]
        split_rows(
            split_dot(pick[...], jnp.concatenate(cyc, axis=1)), face_send.at[step])
        face_recv[step, my_blk] = face_send[step, my_blk]
        each(peers, lambda off: face_copy(step, off, my_blk).start())

        if step == STEPS - 1:
            owner = ints[3:4, :].astype(jnp.int32)
            group = owner // (4 * levs)
            row = (owner // 4) % levs * (4 * peers) + group * 4 + owner % 4
            ids = lax.broadcasted_iota(jnp.int32, (4 * peers * levs, blocks), 0)
            hot = jnp.where(ids == row, 1.0, 0.0).astype(BF16)
            tiles[...] = split_dot(hot, grad[...]).reshape(levs, 4 * peers, cells)
            for off in range(1, levs):
                tile_copy(off, my_lev).start()

        for group in range(blocks // GROUP):
            rows = slice(group * GROUP, (group + 1) * GROUP)
            active = flat_sub[rows, 0:1]

            @pl.loop(0, lev_here)
            def _(level):
                value = x[level, rows, :]
                c0, ce, cn = centre[level, rows, :], east[level, rows, :], north[level, rows, :]
                for substep in range(RMAX):
                    moved = (
                        c0 * value
                        + ce * pltpu.roll(value, cells - 1, 1)
                        + cn * pltpu.roll(value, cells - side, 1))
                    value = jnp.where(active > substep, moved, value)
                x[level, rows, :] = value

        if step == 0:
            each(peers, lambda off: key_copy(off, source_at(off)).wait_recv())
            keys = join_rows(key_recv)
            lane = lax.broadcasted_iota(jnp.int32, (slots, 128), 1).astype(F32)
            place[...] = jnp.where(keys == lane, 1.0, 0.0).T[:blocks].astype(BF16)
        else:
            for off in range(1, levs):
                tile_copy(off, lax.rem(my_lev + levs - off, levs)).wait_recv()
            total = tiles[my_lev]
            for off in range(1, levs):
                total = total + tiles_recv[lax.rem(my_lev + levs - off, levs)]
            for p in range(peers):
                owned[p] = total[4 * p : 4 * p + 4]
            each(peers, lambda off: own_copy(off, my_blk).start())
        each(peers, lambda off: face_copy(step, off, source_at(off)).wait_recv())
        arrived = split_dot(place[...], join_rows(face_recv.at[step]))
        for level in range(lev_here):
            value = x[level] + split_dot(
                arrived[:, level * cycle : (level + 1) * cycle], spread_t[...])
            if step < STEPS - 1:
                x[level] = value
                grad[...] = grad[...] + profile[level] * value
            else:
                out[level] = value

    each(peers, lambda off: own_copy(off, source_at(off)).wait_recv())
    tile_out[...] = owned[my_blk]

    def add_owned(off):
        tile_out[...] = tile_out[...] + owned_recv[source_at(off)]

    each(peers, add_owned)
    for step in range(STEPS):
        finish_solve(step)
        each(peers, lambda off: face_copy(step, off, my_blk).wait_send())
    each(peers, lambda off: key_copy(off, my_blk).wait_send())
    for off in range(1, levs):
        tile_copy(off, my_lev).wait_send()
    each(peers, lambda off: own_copy(off, my_blk).wait_send())


def local(
    adjoint_in,
    courant,
    mixing,
    oh_rate,
    substeps,
    nest_weight,
    dest_device,
    dest_slot,
    emission_profile,
    tile_owner,
):
    blocks, lev_here, cells = adjoint_in.shape
    cycle = nest_weight.shape[1]
    peers = lax.axis_size("blk")
    levs = lax.axis_size("lev")
    cap = min(blocks, 2 * blocks // peers)
    chunk = blocks // CHUNKS
    ints = jnp.stack([substeps, dest_device[:, 0], dest_slot, tile_owner]).astype(F32)
    vmem = pl.BlockSpec(memory_space=pltpu.VMEM)
    whole = pltpu.VMEM((lev_here, blocks, cells), F32)
    line = pltpu.VMEM((STEPS + 1, CHUNKS, chunk, cells), F32)
    dma = pltpu.SemaphoreType.DMA
    out, tile_grad = pl.pallas_call(
        functools.partial(kernel, peers, levs),
        out_shape=(
            jax.ShapeDtypeStruct((lev_here, blocks, cells), F32),
            jax.ShapeDtypeStruct((4, cells), F32),
        ),
        in_specs=[vmem] * 6 + [pl.BlockSpec(memory_space=pltpu.SMEM)],
        out_specs=(vmem, vmem),
        scratch_shapes=[
            whole,
            whole,
            whole,
            whole,
            whole,
            pltpu.VMEM((2 * lev_here, blocks, cells), F32),
            pltpu.VMEM((4, blocks, cells), F32),
            pltpu.VMEM((blocks, cells), F32),
            pltpu.VMEM((cells, cycle), BF16),
            pltpu.VMEM((cycle, cells), BF16),
            pltpu.VMEM((peers * cap, blocks), BF16),
            pltpu.VMEM((blocks, peers * cap), BF16),
            pltpu.VMEM((peers * cap, lev_here * cycle), F32),
            pltpu.VMEM((peers, cap, 128), F32),
            pltpu.VMEM((peers, cap, 128), F32),
            pltpu.VMEM((STEPS, peers, cap, lev_here * cycle), F32),
            pltpu.VMEM((STEPS, peers, cap, lev_here * cycle), F32),
            line,
            line,
            line,
            line,
            line,
            line,
            pltpu.VMEM((levs, 4 * peers, cells), F32),
            pltpu.VMEM((levs, 4 * peers, cells), F32),
            pltpu.VMEM((peers, 4, cells), F32),
            pltpu.VMEM((peers, 4, cells), F32),
            dma((STEPS + 1, CHUNKS)),
            dma((STEPS + 1, CHUNKS)),
            dma((STEPS + 1, CHUNKS)),
            dma((STEPS + 1, CHUNKS)),
            dma((STEPS, CHUNKS)),
            dma((STEPS, CHUNKS)),
            dma((peers,)),
            dma((peers,)),
            dma((STEPS, peers)),
            dma((STEPS, peers)),
            dma((levs,)),
            dma((levs,)),
            dma((peers,)),
            dma((peers,)),
        ],
        compiler_params=pltpu.CompilerParams(
            collective_id=0, has_side_effects=True, vmem_limit_bytes=56 * 1024 * 1024
        ),
    )(
        jnp.transpose(adjoint_in, (1, 0, 2)),
        jnp.transpose(courant, (0, 2, 1, 3)),
        jnp.transpose(mixing, (1, 0, 2)),
        jnp.transpose(oh_rate, (1, 0, 2)),
        ints,
        nest_weight,
        emission_profile,
    )
    return jnp.transpose(out, (1, 0, 2)), tile_grad


def solution(mesh):
    placed = (
        P("blk", "lev", None),
        P(None, "blk", "lev", None),
        P("blk", "lev", None),
        P("blk", "lev", None),
        P("blk"),
        P("blk", None),
        P("blk", None),
        P("blk"),
        P("lev"),
        P("blk"),
    )
    return jax.shard_map(
        local,
        mesh=mesh,
        in_specs=placed,
        out_specs=(P("blk", "lev", None), P(("blk", "lev"), None)),
        check_vma=False,
    )
```

time: 420 us -> 54 us (0.13)
  waiting for transfers between devices: 147 us -> 0 us
  blocking collectives: 87.2 us -> 0 us
  local copies, waits for them, and re-layouts: 89.2 us -> 2.7 us
  other arithmetic: 53.3 us -> 1.29 us
  Pallas kernels: 0 us -> 49.2 us
  starting transfers between devices: 21.2 us -> 0 us
  between operations: 15.3 us -> 0.65 us
    unnamed x2 -> x0, waiting for transfers between devices: 129 us -> none
    all_gather x2 -> x0, blocking collectives: 64.7 us -> none  [route_cycles(): lax.all_gather(cycle_flat, 'blk', axis=0, tiled=True)]
    pallas_call x0 -> x1, Pallas kernels: none -> 49.2 us  [local(): pl.pallas_call(functools.partial(kernel, peers, levs), out_shape=(jax.Sha...]
    unnamed x98 -> x4, local copies, waits for them, and re-layouts: 37.3 us -> 2.7 us
    unnamed x1 -> x0, blocking collectives: 22.5 us -> none
    all_to_all x5 -> x0, starting transfers between devices: 21.2 us -> none  [the longest x2 8.61 us: local(): lax.all_to_all(adjoint * survive, 'lev', split_axis=2, concat_axis=1, til...]
    slice x24 -> x0, local copies, waits for them, and re-layouts: 18.2 us -> none  [the longest x9 5.18 us: stencil(): north_adj = jnp.concatenate([grid_view[..., 1:, :], zero_row], axis=-2)]
    all_to_all x5 -> x0, waiting for transfers between devices: 17.9 us -> none  [the longest x2 14.3 us: local(): lax.all_to_all(adjoint * survive, 'lev', split_axis=2, concat_axis=1, til...]
  transfers between devices with their start and end apart: 6 -> 0, of which waited for: 4 -> 0; matrix products, arithmetic and copies ran while one was open for 6% -> 0% of each run, Pallas kernels for 0% -> 0%
where the time goes in v1:
time: 54 us; the launch traced here: 53.9 us
  Pallas kernels  49.2 us (91%)
  local copies, waits for them, and re-layouts  2.7 us (5%)
  other arithmetic  1.29 us (2%)
  between operations  0.65 us (1%)
    pallas_call x1, Pallas kernels, local(): pl.pallas_call(functools.partial(kernel, peers, levs), out_shape=(jax.Sha...  49.2 us
    unnamed x4, local copies, waits for them, and re-layouts  2.7 us
    convert_element_type x1, other arithmetic, local(): jnp.stack([substeps, dest_device[:, 0], dest_slot, tile_owner]).astype(F32)  1.29 us

profile of v1, /device:TPU:0, one launch (start us, length us, event | category | flops | bytes accessed | tf_op | source)
XLA Modules:
  0.0 53.9 jit_solution(9731284886773203670)
XLA Ops:
  0.6 1.3 %add_convert_fusion.ints = f32[4,64]{1,0:T(4,128)} fusion(s32[1,64]{1,0:T(1,128)} %bitcast.14, s32[1,64]{1,0:T(1,128)} %bitcast.15, s32[1,64]{1,0:T(1,128)} %bitcast.16, s32[1,64]{1,0:T(1,128)} %bitcast.17), kind=kLoop, calls=%fused_computation | loop fusion | flops 1024 | bytes 2048 | tf_op jit(solution)/shard_map/convert_element_type | solution.py:509
  1.9 49.2 %shard_map.113 = (f32[3,64,1024]{2,1,0:T(8,128)}, f32[4,1024]{1,0:T(4,128)}) custom-call(f32[3,64,1024]{2,1,0:T(8,128)} %bitcast.11, f32[2,3,64,1024]{3,2,1,0:T(8,128)} %bitcast.9, f32[3,64,1024]{2,1,0:T(8,128)} %bitcast.12, f32[3,64,1024]{2,1,0:T(8,128)} %bitcast.13, f32[4,64]{1,0:T(4,128)} %add_convert_fusion.ints, f32[64,128]{1,0:T(8,128)} %weight.1, ...), custom_call_target="tpu_custom_call" | custom-call | tf_op jit(solution)/shard_map/pallas_call | solution.py:514
  51.2 0.0 copy-start
  51.2 2.1 %copy.14 = f32[64,3,1024]{2,0,1:T(8,128)} copy(f32[64,3,1024]{2,0,1:T(8,128)} %bitcast.10) | data formatting | bytes 1572864
  53.3 0.0 copy-done
  53.3 0.6 %copy.15 = f32[4,1024]{1,0:T(4,128)} copy(f32[4,1024]{1,0:T(4,128)S(1)} %copy-done) | data formatting | bytes 32768
Async XLA Ops:
  51.2 2.1 %copy-start = (f32[4,1024]{1,0:T(4,128)S(1)}, f32[4,1024]{1,0:T(4,128)}, u32[]{:S(2)}) copy-start(f32[4,1024]{1,0:T(4,128)} %get-tuple-element.9) | copy-start | bytes 49156

commit v2 on v1

--- a/solution.py
+++ b/solution.py
@@ -10,7 +10,7 @@
 RMAX = 4
 STEPS = 2
 CHUNKS = 4
-GROUP = 8
+GROUP = 16
 MESH = pl.DeviceIdType.MESH
 F32 = jnp.float32
 BF16 = jnp.bfloat16
@@ -24,9 +24,11 @@
         high = right.astype(BF16)
         low = (right - high.astype(F32)).astype(BF16)
         return run(left, high) + run(left, low)
+    rows = left.shape[0]
     high = left.astype(BF16)
     low = (left - high.astype(F32)).astype(BF16)
-    return run(high, right) + run(low, right)
+    both = run(jnp.concatenate([high, low], axis=0), right)
+    return both[:rows] + both[rows:]
 
 
 def each(count, body):
@@ -40,16 +42,26 @@
 def kernel(
     peers,
     levs,
-    adj,
+    adj_far,
     courant,
-    mix,
-    oh,
-    ints,
+    mix_far,
+    oh_far,
+    substeps,
+    dest_device,
+    dest_slot,
+    tile_owner,
     weight,
     profile,
     out,
     tile_out,
     surv,
+    adj,
+    mix,
+    oh,
+    courant_here,
+    load_sems,
+    store_sems,
+    sub_wide,
     centre,
     east,
     north,
@@ -91,7 +103,7 @@
     own_ss,
     own_rs,
 ):
-    lev_here, blocks, cells = adj.shape
+    lev_here, blocks, cells = adj_far.shape
     cycle = weight.shape[1]
     side = cycle // 4
     cap = key_send.shape[1]
@@ -108,6 +120,14 @@
     def source_at(off):
         return lax.rem(my_blk + peers - off, peers)
 
+    loads = [
+        pltpu.make_async_copy(source, target, load_sems.at[n])
+        for n, (source, target) in enumerate(
+            [(oh_far, oh), (adj_far, adj), (mix_far, mix), (courant, courant_here)])
+    ]
+    fetch = loads[-1]
+    for load in loads:
+        load.start()
     barrier = pltpu.get_barrier_semaphore()
     each(peers, lambda off: pl.semaphore_signal(
         barrier, inc=1, device_id=(peer_at(off), my_lev), device_id_type=MESH))
@@ -185,6 +205,127 @@
 
     def send_rows(item):
         return pl.ds(pl.multiple_of(item * GROUP, GROUP), GROUP)
+
+    def key_copy(off, whose):
+        return pltpu.make_async_remote_copy(
+            key_send.at[peer_at(off)], key_recv.at[whose], key_ss.at[off], key_rs.at[off],
+            device_id=(peer_at(off), my_lev), device_id_type=MESH)
+
+    def face_copy(step, off, whose):
+        return pltpu.make_async_remote_copy(
+            face_send.at[step, peer_at(off)], face_recv.at[step, whose],
+            face_ss.at[step, off], face_rs.at[step, off],
+            device_id=(peer_at(off), my_lev), device_id_type=MESH)
+
+    def pair_copy(which, target):
+        return pltpu.make_async_remote_copy(
+            tiles.at[target], tiles_recv.at[which], tile_ss.at[which], tile_rs.at[which],
+            device_id=(my_blk, partner), device_id_type=MESH)
+
+    def pair_copies():
+        return [pair_copy(0, partner), pair_copy(1, levs - 1 - partner)]
+
+    def far_copy():
+        return pltpu.make_async_remote_copy(
+            tiles.at[across], tiles_recv.at[2], tile_ss.at[2], tile_rs.at[2],
+            device_id=(my_blk, across), device_id_type=MESH)
+
+    def send_tiles():
+        owner = tile_owner[...]
+        group = owner // (4 * levs)
+        row = (owner // 4) % levs * (4 * peers) + group * 4 + owner % 4
+        ids = lax.broadcasted_iota(jnp.int32, (4 * peers * levs, blocks), 0)
+        hot = jnp.where(ids == row, 1.0, 0.0).astype(BF16)
+        tiles[...] = split_dot(hot, grad[...]).reshape(levs, 4 * peers, cells)
+        for copy in pair_copies():
+            copy.start()
+
+    def own_copy(off, whose):
+        return pltpu.make_async_remote_copy(
+            owned.at[peer_at(off)], owned_recv.at[whose], own_ss.at[off], own_rs.at[off],
+            device_id=(peer_at(off), my_lev), device_id_type=MESH)
+
+    def split_rows(value, target):
+        width = value.shape[1]
+        if cap % 8 == 0:
+            target[...] = value.reshape(peers, cap, width)
+        else:
+            flat[:, :width] = value
+            for p in range(peers):
+                target[p] = flat[p * cap : (p + 1) * cap, :width]
+
+    def join_rows(source):
+        width = source.shape[-1]
+        if cap % 8 == 0:
+            return source[...].reshape(slots, width)
+        for p in range(peers):
+            flat[p * cap : (p + 1) * cap, :width] = source[p]
+        return flat[:, :width]
+
+    def prepare_routes():
+        eye = (
+            lax.broadcasted_iota(jnp.int32, (blocks, blocks), 0)
+            == lax.broadcasted_iota(jnp.int32, (blocks, blocks), 1)
+        )
+
+        def column(row):
+            return jnp.sum(jnp.where(eye, row, 0.0), axis=1, keepdims=True)
+
+        dest = dest_device[...].astype(F32)
+        same = jnp.logical_and(
+            column(dest) == dest,
+            lax.broadcasted_iota(jnp.int32, (blocks, blocks), 0)
+            < lax.broadcasted_iota(jnp.int32, (blocks, blocks), 1),
+        )
+        rank = jnp.sum(jnp.where(same, 1.0, 0.0), axis=0, keepdims=True)
+        slot_row = dest * cap + rank
+        slot_id = lax.broadcasted_iota(jnp.int32, (slots, blocks), 0).astype(F32)
+        pick[...] = jnp.where(slot_id == slot_row, 1.0, 0.0).astype(BF16)
+        keys = column(dest_slot[...].astype(F32)) + jnp.zeros((blocks, 128), F32)
+        split_rows(
+            jnp.dot(pick[...], keys.astype(BF16), preferred_element_type=F32), key_send)
+        key_recv[my_blk] = key_send[my_blk]
+        each(peers, lambda off: key_copy(off, my_blk).start())
+
+        face = lax.broadcasted_iota(jnp.int32, (cycle, cells), 0)
+        cell = lax.broadcasted_iota(jnp.int32, (cycle, cells), 1)
+        wanted = jnp.where(
+            face < side, face,
+            jnp.where(
+                face < 2 * side, face + (cells - 2 * side),
+                jnp.where(
+                    face < 3 * side, (face - 2 * side) * side,
+                    (face - 3 * side) * side + side - 1)))
+        spread_t[...] = jnp.where(cell == wanted, 1.0, 0.0).astype(BF16)
+        face = lax.broadcasted_iota(jnp.int32, (cells, cycle), 1)
+        cell = lax.broadcasted_iota(jnp.int32, (cells, cycle), 0)
+        wanted = jnp.where(
+            face < side, face,
+            jnp.where(
+                face < 2 * side, face + (cells - 2 * side),
+                jnp.where(
+                    face < 3 * side, (face - 2 * side) * side,
+                    (face - 3 * side) * side + side - 1)))
+        gather_t[...] = jnp.where(cell == wanted, 1.0, 0.0).astype(BF16)
+
+        sub_wide[...] = column(substeps[...].astype(F32)) + jnp.zeros((blocks, 128), F32)
+
+    def prepare_stencil():
+        fetch.wait()
+
+        @pl.loop(0, blocks // GROUP)
+        def _(item):
+            rows = pl.ds(pl.multiple_of(item * GROUP, GROUP), GROUP)
+            cell = lax.broadcasted_iota(jnp.int32, (GROUP, cells), 1)
+            total = jnp.zeros((GROUP, cells), F32)
+            for level in range(lev_here):
+                e, n = courant_here[0, level, rows, :], courant_here[1, level, rows, :]
+                centre[level, rows, :] = 1.0 - e - n
+                east[level, rows, :] = jnp.where((cell & (side - 1)) == side - 1, 0.0, e)
+                north[level, rows, :] = jnp.where(cell >= cells - side, 0.0, n)
+                total = total + profile[level] * adj[level, rows, :]
+            grad[rows, :] = total
+
 
     def solve(step):
         @pl.when(outer)
@@ -208,6 +349,11 @@
                 if step == 0:
                     first_line(part, partner).start()
                 line_copy(step, part, partner).start()
+            if step == 0:
+                prepare_routes()
+                prepare_stencil()
+            else:
+                send_tiles()
             for part in range(CHUNKS):
                 back_copy(step, part, partner).wait_recv()
 
@@ -220,6 +366,8 @@
 
         @pl.when(jnp.logical_not(outer))
         def _():
+            if step == 0:
+                prepare_routes()
             for part in range(CHUNKS):
                 if step == 0:
                     first_line(part, partner).wait_recv()
@@ -254,6 +402,10 @@
                 if step == 0:
                     cross_copy(STEPS, part, across).start()
                 cross_copy(step, part, across).start()
+            if step == 0:
+                prepare_stencil()
+            else:
+                send_tiles()
             for part in range(CHUNKS):
                 if step == 0:
                     cross_copy(STEPS, part, across).wait_recv()
@@ -295,44 +447,8 @@
                 cross_copy(step, part, across).wait_send()
                 back_copy(step, part, partner).wait_send()
 
-    def key_copy(off, whose):
-        return pltpu.make_async_remote_copy(
-            key_send.at[peer_at(off)], key_recv.at[whose], key_ss.at[off], key_rs.at[off],
-            device_id=(peer_at(off), my_lev), device_id_type=MESH)
-
-    def face_copy(step, off, whose):
-        return pltpu.make_async_remote_copy(
-            face_send.at[step, peer_at(off)], face_recv.at[step, whose],
-            face_ss.at[step, off], face_rs.at[step, off],
-            device_id=(peer_at(off), my_lev), device_id_type=MESH)
-
-    def tile_copy(off, whose):
-        target = lax.rem(my_lev + off, levs)
-        return pltpu.make_async_remote_copy(
-            tiles.at[target], tiles_recv.at[whose], tile_ss.at[off], tile_rs.at[off],
-            device_id=(my_blk, target), device_id_type=MESH)
-
-    def own_copy(off, whose):
-        return pltpu.make_async_remote_copy(
-            owned.at[peer_at(off)], owned_recv.at[whose], own_ss.at[off], own_rs.at[off],
-            device_id=(peer_at(off), my_lev), device_id_type=MESH)
-
-    def split_rows(value, target):
-        width = value.shape[1]
-        if cap % 8 == 0:
-            target[...] = value.reshape(peers, cap, width)
-        else:
-            flat[:, :width] = value
-            for p in range(peers):
-                target[p] = flat[p * cap : (p + 1) * cap, :width]
-
-    def join_rows(source):
-        width = source.shape[-1]
-        if cap % 8 == 0:
-            return source[...].reshape(slots, width)
-        for p in range(peers):
-            flat[p * cap : (p + 1) * cap, :width] = source[p]
-        return flat[:, :width]
+    for load in loads[:-1]:
+        load.wait()
 
     @pl.loop(0, blocks // GROUP)
     def _(item):
@@ -343,109 +459,36 @@
 
     pl.semaphore_wait(barrier, peers - 1 + levs - 1)
 
-    def prepare():
-        eye = (
-            lax.broadcasted_iota(jnp.int32, (blocks, blocks), 0)
-            == lax.broadcasted_iota(jnp.int32, (blocks, blocks), 1)
-        )
-
-        def column(row):
-            return jnp.sum(jnp.where(eye, row, 0.0), axis=1, keepdims=True)
-
-        dest = ints[1:2, :]
-        same = jnp.logical_and(
-            column(dest) == dest,
-            lax.broadcasted_iota(jnp.int32, (blocks, blocks), 0)
-            < lax.broadcasted_iota(jnp.int32, (blocks, blocks), 1),
-        )
-        rank = jnp.sum(jnp.where(same, 1.0, 0.0), axis=0, keepdims=True)
-        slot_row = dest * cap + rank
-        slot_id = lax.broadcasted_iota(jnp.int32, (slots, blocks), 0).astype(F32)
-        pick[...] = jnp.where(slot_id == slot_row, 1.0, 0.0).astype(BF16)
-        keys = column(ints[2:3, :]) + jnp.zeros((blocks, 128), F32)
-        split_rows(
-            jnp.dot(pick[...], keys.astype(BF16), preferred_element_type=F32), key_send)
-        key_recv[my_blk] = key_send[my_blk]
-        each(peers, lambda off: key_copy(off, my_blk).start())
-
-        face = lax.broadcasted_iota(jnp.int32, (cycle, cells), 0)
-        cell = lax.broadcasted_iota(jnp.int32, (cycle, cells), 1)
-        wanted = jnp.where(
-            face < side, face,
-            jnp.where(
-                face < 2 * side, face + (cells - 2 * side),
-                jnp.where(
-                    face < 3 * side, (face - 2 * side) * side,
-                    (face - 3 * side) * side + side - 1)))
-        spread_t[...] = jnp.where(cell == wanted, 1.0, 0.0).astype(BF16)
-        face = lax.broadcasted_iota(jnp.int32, (cells, cycle), 1)
-        cell = lax.broadcasted_iota(jnp.int32, (cells, cycle), 0)
-        wanted = jnp.where(
-            face < side, face,
-            jnp.where(
-                face < 2 * side, face + (cells - 2 * side),
-                jnp.where(
-                    face < 3 * side, (face - 2 * side) * side,
-                    (face - 3 * side) * side + side - 1)))
-        gather_t[...] = jnp.where(cell == wanted, 1.0, 0.0).astype(BF16)
-
-        @pl.loop(0, blocks // GROUP)
-        def _(item):
-            rows = pl.ds(pl.multiple_of(item * GROUP, GROUP), GROUP)
-            cell = lax.broadcasted_iota(jnp.int32, (GROUP, cells), 1)
-            total = jnp.zeros((GROUP, cells), F32)
-            for level in range(lev_here):
-                e, n = courant[0, level, rows, :], courant[1, level, rows, :]
-                centre[level, rows, :] = 1.0 - e - n
-                east[level, rows, :] = jnp.where(cell % side == side - 1, 0.0, e)
-                north[level, rows, :] = jnp.where(cell >= cells - side, 0.0, n)
-                total = total + profile[level] * adj[level, rows, :]
-            grad[rows, :] = total
-
-        return column(ints[0:1, :])
-
-    solve(0)
-    sub_column = prepare()
-    sub_wide = sub_column + jnp.zeros((blocks, 128), F32)
-    place_ready = False
-    flat_sub = sub_wide
-
     for step in range(STEPS):
-        if step > 0:
-            solve(step)
-        cyc = [
-            split_dot(x[level], gather_t[...]) * weight[...] for level in range(lev_here)
-        ]
-        split_rows(
-            split_dot(pick[...], jnp.concatenate(cyc, axis=1)), face_send.at[step])
+        solve(step)
+        cyc = split_dot(
+            jnp.concatenate([x[level] for level in range(lev_here)], axis=0), gather_t[...])
+        cyc = jnp.concatenate(
+            [cyc[level * blocks : (level + 1) * blocks] * weight[...] for level in range(lev_here)],
+            axis=1)
+        split_rows(split_dot(pick[...], cyc), face_send.at[step])
         face_recv[step, my_blk] = face_send[step, my_blk]
         each(peers, lambda off: face_copy(step, off, my_blk).start())
 
         if step == STEPS - 1:
-            owner = ints[3:4, :].astype(jnp.int32)
-            group = owner // (4 * levs)
-            row = (owner // 4) % levs * (4 * peers) + group * 4 + owner % 4
-            ids = lax.broadcasted_iota(jnp.int32, (4 * peers * levs, blocks), 0)
-            hot = jnp.where(ids == row, 1.0, 0.0).astype(BF16)
-            tiles[...] = split_dot(hot, grad[...]).reshape(levs, 4 * peers, cells)
-            for off in range(1, levs):
-                tile_copy(off, my_lev).start()
-
-        for group in range(blocks // GROUP):
-            rows = slice(group * GROUP, (group + 1) * GROUP)
-            active = flat_sub[rows, 0:1]
-
-            @pl.loop(0, lev_here)
-            def _(level):
-                value = x[level, rows, :]
-                c0, ce, cn = centre[level, rows, :], east[level, rows, :], north[level, rows, :]
-                for substep in range(RMAX):
-                    moved = (
-                        c0 * value
-                        + ce * pltpu.roll(value, cells - 1, 1)
-                        + cn * pltpu.roll(value, cells - side, 1))
-                    value = jnp.where(active > substep, moved, value)
-                x[level, rows, :] = value
+            for copy in pair_copies():
+                copy.wait_send()
+                copy.wait_recv()
+            tiles[across] = tiles[across] + tiles_recv[1]
+            far_copy().start()
+
+        active = sub_wide[:, 0:1]
+
+        @pl.loop(0, lev_here)
+        def _(level):
+            value = x[level]
+            for substep in range(RMAX):
+                moved = (
+                    centre[level] * value
+                    + east[level] * pltpu.roll(value, cells - 1, 1)
+                    + north[level] * pltpu.roll(value, cells - side, 1))
+                value = jnp.where(active > substep, moved, value)
+            x[level] = value
 
         if step == 0:
             each(peers, lambda off: key_copy(off, source_at(off)).wait_recv())
@@ -453,24 +496,26 @@
             lane = lax.broadcasted_iota(jnp.int32, (slots, 128), 1).astype(F32)
             place[...] = jnp.where(keys == lane, 1.0, 0.0).T[:blocks].astype(BF16)
         else:
-            for off in range(1, levs):
-                tile_copy(off, lax.rem(my_lev + levs - off, levs)).wait_recv()
-            total = tiles[my_lev]
-            for off in range(1, levs):
-                total = total + tiles_recv[lax.rem(my_lev + levs - off, levs)]
+            far_copy().wait_recv()
+            total = tiles[my_lev] + tiles_recv[0] + tiles_recv[2]
             for p in range(peers):
                 owned[p] = total[4 * p : 4 * p + 4]
             each(peers, lambda off: own_copy(off, my_blk).start())
         each(peers, lambda off: face_copy(step, off, source_at(off)).wait_recv())
         arrived = split_dot(place[...], join_rows(face_recv.at[step]))
+        spread = split_dot(
+            jnp.concatenate(
+                [arrived[:, level * cycle : (level + 1) * cycle] for level in range(lev_here)],
+                axis=0),
+            spread_t[...])
         for level in range(lev_here):
-            value = x[level] + split_dot(
-                arrived[:, level * cycle : (level + 1) * cycle], spread_t[...])
+            value = x[level] + spread[level * blocks : (level + 1) * blocks]
             if step < STEPS - 1:
                 x[level] = value
                 grad[...] = grad[...] + profile[level] * value
             else:
-                out[level] = value
+                x[level] = value
+                pltpu.make_async_copy(x.at[level], out.at[level], store_sems.at[level]).start()
 
     each(peers, lambda off: own_copy(off, source_at(off)).wait_recv())
     tile_out[...] = owned[my_blk]
@@ -479,13 +524,19 @@
         tile_out[...] = tile_out[...] + owned_recv[source_at(off)]
 
     each(peers, add_owned)
+    for level in range(lev_here):
+        pltpu.make_async_copy(x.at[level], out.at[level], store_sems.at[level]).wait()
     for step in range(STEPS):
         finish_solve(step)
         each(peers, lambda off: face_copy(step, off, my_blk).wait_send())
     each(peers, lambda off: key_copy(off, my_blk).wait_send())
-    for off in range(1, levs):
-        tile_copy(off, my_lev).wait_send()
+    far_copy().wait_send()
     each(peers, lambda off: own_copy(off, my_blk).wait_send())
+
+
+def emit(field, tile_rows, out, tile_out):
+    out[...] = field[...]
+    tile_out[...] = tile_rows[...]
 
 
 def local(
@@ -506,7 +557,6 @@
     levs = lax.axis_size("lev")
     cap = min(blocks, 2 * blocks // peers)
     chunk = blocks // CHUNKS
-    ints = jnp.stack([substeps, dest_device[:, 0], dest_slot, tile_owner]).astype(F32)
     vmem = pl.BlockSpec(memory_space=pltpu.VMEM)
     whole = pltpu.VMEM((lev_here, blocks, cells), F32)
     line = pltpu.VMEM((STEPS + 1, CHUNKS, chunk, cells), F32)
@@ -517,10 +567,18 @@
             jax.ShapeDtypeStruct((lev_here, blocks, cells), F32),
             jax.ShapeDtypeStruct((4, cells), F32),
         ),
-        in_specs=[vmem] * 6 + [pl.BlockSpec(memory_space=pltpu.SMEM)],
-        out_specs=(vmem, vmem),
+        in_specs=[pl.BlockSpec(memory_space=pl.ANY)] * 4 + [vmem] * 5
+        + [pl.BlockSpec(memory_space=pltpu.SMEM)],
+        out_specs=(pl.BlockSpec(memory_space=pl.ANY), vmem),
         scratch_shapes=[
             whole,
+            whole,
+            whole,
+            whole,
+            pltpu.VMEM((2, lev_here, blocks, cells), F32),
+            dma((4,)),
+            dma((lev_here,)),
+            pltpu.VMEM((blocks, 128), F32),
             whole,
             whole,
             whole,
@@ -544,7 +602,7 @@
             line,
             line,
             pltpu.VMEM((levs, 4 * peers, cells), F32),
-            pltpu.VMEM((levs, 4 * peers, cells), F32),
+            pltpu.VMEM((3, 4 * peers, cells), F32),
             pltpu.VMEM((peers, 4, cells), F32),
             pltpu.VMEM((peers, 4, cells), F32),
             dma((STEPS + 1, CHUNKS)),
@@ -563,17 +621,29 @@
             dma((peers,)),
         ],
         compiler_params=pltpu.CompilerParams(
-            collective_id=0, has_side_effects=True, vmem_limit_bytes=56 * 1024 * 1024
+            collective_id=0, has_side_effects=True, vmem_limit_bytes=60 * 1024 * 1024
         ),
     )(
         jnp.transpose(adjoint_in, (1, 0, 2)),
         jnp.transpose(courant, (0, 2, 1, 3)),
         jnp.transpose(mixing, (1, 0, 2)),
         jnp.transpose(oh_rate, (1, 0, 2)),
-        ints,
+        substeps.reshape(1, blocks),
+        dest_device.reshape(1, blocks),
+        dest_slot.reshape(1, blocks),
+        tile_owner.reshape(1, blocks),
         nest_weight,
         emission_profile,
     )
+    out, tile_grad = pl.pallas_call(
+        emit,
+        out_shape=(
+            jax.ShapeDtypeStruct(out.shape, F32),
+            jax.ShapeDtypeStruct(tile_grad.shape, F32),
+        ),
+        in_specs=[vmem, vmem],
+        out_specs=(vmem, vmem),
+    )(out, tile_grad)
     return jnp.transpose(out, (1, 0, 2)), tile_grad
 
 

time: 54 us -> 45.4 us (0.84)
  Pallas kernels: 49.2 us -> 44.6 us
  local copies, waits for them, and re-layouts: 2.7 us -> 0 us
  other arithmetic: 1.29 us -> 0 us
    pallas_call x1, Pallas kernels: 49.2 us -> 42.5 us  [local(): pl.pallas_call(functools.partial(kernel, peers, levs), out_shape=(jax.Sha...]
    unnamed x4 -> x0, local copies, waits for them, and re-layouts: 2.7 us -> none
    pallas_call x0 -> x1, Pallas kernels: none -> 2.07 us  [local(): pl.pallas_call(emit, out_shape=(jax.ShapeDtypeStruct(out.shape, F32), jax...]
    convert_element_type x1 -> x0, other arithmetic: 1.29 us -> none  [local(): jnp.stack([substeps, dest_device[:, 0], dest_slot, tile_owner]).astype(F32)]
where the time goes in v2:
time: 45.4 us; the launch traced here: 45.2 us
  Pallas kernels  44.6 us (98%)
  between operations  0.64 us (1%)
    pallas_call x1, Pallas kernels, local(): pl.pallas_call(functools.partial(kernel, peers, levs), out_shape=(jax.Sha...  42.5 us
    pallas_call x1, Pallas kernels, local(): pl.pallas_call(emit, out_shape=(jax.ShapeDtypeStruct(out.shape, F32), jax...  2.07 us

profile of v2, /device:TPU:0, one launch (start us, length us, event | category | flops | bytes accessed | tf_op | source)
XLA Modules:
  0.0 45.2 jit_solution(11179883527437963913)
XLA Ops:
  0.6 42.5 %shard_map.113 = (f32[3,64,1024]{2,1,0:T(8,128)}, f32[4,1024]{1,0:T(4,128)}) custom-call(f32[3,64,1024]{2,1,0:T(8,128)} %bitcast.10, f32[2,3,64,1024]{3,2,1,0:T(8,128)} %bitcast.9, f32[3,64,1024]{2,1,0:T(8,128)} %bitcast.11, f32[3,64,1024]{2,1,0:T(8,128)} %bitcast.12, s32[1,64]{1,0:T(1,128)} %bitcast.13, s32[1,64]{1,0:T(1,128)} %bitcast.14, ...), custom_call_target="tpu_custom_call" | custom-call | tf_op jit(solution)/shard_map/pallas_call | solution.py:564
  43.1 2.1 %shard_map.114 = (f32[3,64,1024]{2,1,0:T(8,128)}, f32[4,1024]{1,0:T(4,128)}) custom-call(f32[3,64,1024]{2,1,0:T(8,128)} %get-tuple-element.6.field, f32[4,1024]{1,0:T(4,128)} %get-tuple-element.7.tile_rows), custom_call_target="tpu_custom_call" | custom-call | tf_op jit(solution)/shard_map/pallas_call | solution.py:638

commit v3 on v2

--- a/solution.py
+++ b/solution.py
@@ -461,6 +461,13 @@
 
     for step in range(STEPS):
         solve(step)
+        if step == STEPS - 1:
+            for copy in pair_copies():
+                copy.wait_send()
+                copy.wait_recv()
+            tiles[across] = tiles[across] + tiles_recv[1]
+            far_copy().start()
+
         cyc = split_dot(
             jnp.concatenate([x[level] for level in range(lev_here)], axis=0), gather_t[...])
         cyc = jnp.concatenate(
@@ -469,13 +476,6 @@
         split_rows(split_dot(pick[...], cyc), face_send.at[step])
         face_recv[step, my_blk] = face_send[step, my_blk]
         each(peers, lambda off: face_copy(step, off, my_blk).start())
-
-        if step == STEPS - 1:
-            for copy in pair_copies():
-                copy.wait_send()
-                copy.wait_recv()
-            tiles[across] = tiles[across] + tiles_recv[1]
-            far_copy().start()
 
         active = sub_wide[:, 0:1]
 

time: 45.4 us -> 44.7 us (0.985)
  Pallas kernels: 44.6 us -> 43.8 us
    pallas_call x1, Pallas kernels: 42.5 us -> 41.7 us  [local(): pl.pallas_call(functools.partial(kernel, peers, levs), out_shape=(jax.Sha...]
where the time goes in v3:
time: 44.7 us; the launch traced here: 44.4 us
  Pallas kernels  43.8 us (98%)
  between operations  0.64 us (1%)
    pallas_call x1, Pallas kernels, local(): pl.pallas_call(functools.partial(kernel, peers, levs), out_shape=(jax.Sha...  41.7 us
    pallas_call x1, Pallas kernels, local(): pl.pallas_call(emit, out_shape=(jax.ShapeDtypeStruct(out.shape, F32), jax...  2.07 us

profile of v3, /device:TPU:0, one launch (start us, length us, event | category | flops | bytes accessed | tf_op | source)
XLA Modules:
  0.0 44.4 jit_solution(17252681570796908611)
XLA Ops:
  0.6 41.7 %shard_map.113 = (f32[3,64,1024]{2,1,0:T(8,128)}, f32[4,1024]{1,0:T(4,128)}) custom-call(f32[3,64,1024]{2,1,0:T(8,128)} %bitcast.10, f32[2,3,64,1024]{3,2,1,0:T(8,128)} %bitcast.9, f32[3,64,1024]{2,1,0:T(8,128)} %bitcast.11, f32[3,64,1024]{2,1,0:T(8,128)} %bitcast.12, s32[1,64]{1,0:T(1,128)} %bitcast.13, s32[1,64]{1,0:T(1,128)} %bitcast.14, ...), custom_call_target="tpu_custom_call" | custom-call | tf_op jit(solution)/shard_map/pallas_call | solution.py:564
  42.4 2.1 %shard_map.114 = (f32[3,64,1024]{2,1,0:T(8,128)}, f32[4,1024]{1,0:T(4,128)}) custom-call(f32[3,64,1024]{2,1,0:T(8,128)} %get-tuple-element.6.field, f32[4,1024]{1,0:T(4,128)} %get-tuple-element.7.tile_rows), custom_call_target="tpu_custom_call" | custom-call | tf_op jit(solution)/shard_map/pallas_call | solution.py:638
